TPU v7x, 32 devices: a whole 2x2x4 slice. The times are simulated.
32 devices in a mesh: row: 8 (over z, y), col: 4 (over x, core).
Axes of the slice: x: 2, y: 2, z: 4, core: 2. Of those that a mesh axis runs over, the one named last changes fastest.
Arguments:
- gradients: bfloat16 [2, 32768, 16384], P(None, 'row', 'col'), may hold values from -17 to 17
- sketch_matrix: bfloat16 [16384, 256], P('col'), may hold values from -0.046875 to 0.046875
Outputs:
- projector: bfloat16 [2, 32768, 256], P(None, ('row', 'col'))
- projected: float32 [256, 2, 16384], P('row', None, 'col')
All inputs are finite; a program needn't handle non-finite values.
Results may differ from a plain program's by a relative error of at most 0.01.
Values may be sent and summed in bfloat16 or wider, within the bound.
A program may use at most 192 MiB of HBM per device.

v0:
```python
import math

import jax
import jax.numpy as jnp
from jax import lax
from jax.sharding import PartitionSpec as P


def invert_low(factor_low):
    identity = jnp.eye(factor_low.shape[-1], dtype=jnp.float32)
    return jax.vmap(lambda matrix: jax.scipy.linalg.solve_triangular(matrix, identity, lower=True))(
        factor_low
    )


def body(gradients, sketch_matrix):
    rows_here = gradients.shape[1]
    total_rows = rows_here * lax.axis_size("row")
    partial_sketch = jnp.einsum(
        "mrd,dk->mrk", gradients, sketch_matrix, preferred_element_type=jnp.float32
    )
    summed = lax.psum(partial_sketch, "col")
    sketch_rows = summed.astype(jnp.bfloat16)
    portion = rows_here // lax.axis_size("col")
    own_rows = lax.dynamic_slice_in_dim(sketch_rows, lax.axis_index("col") * portion, portion, 1)
    local_gram = jnp.einsum(
        "mrk,mrl->mkl", sketch_rows, sketch_rows, preferred_element_type=jnp.float32
    )
    gram_sum = lax.psum(local_gram, "row")
    factor_low = jnp.linalg.cholesky(gram_sum / total_rows)
    inverse_low = invert_low(factor_low)
    projector = jnp.einsum(
        "mrk,mlk->mrl", own_rows.astype(jnp.float32), inverse_low, precision=lax.Precision.HIGHEST
    ).astype(jnp.bfloat16)
    moment = jnp.einsum("mrk,mrd->mkd", sketch_rows, gradients, preferred_element_type=jnp.float32)
    scaling = 1.0 / math.sqrt(total_rows)
    projected = lax.psum_scatter(
        (
            jnp.einsum("mck,mkd->cmd", inverse_low, moment, precision=lax.Precision.HIGHEST)
            * scaling
        ).astype(jnp.bfloat16),
        "row",
        scatter_dimension=0,
        tiled=True,
    ).astype(jnp.float32)
    return (projector, projected)


def solution(mesh):
    in_specs = (P(None, "row", "col"), P("col", None))
    out_specs = (P(None, ("row", "col"), None), P("row", None, "col"))
    return jax.shard_map(body, mesh=mesh, in_specs=in_specs, out_specs=out_specs, check_vma=False)
```

profile of v0, /device:TPU:0, one launch (start us, length us, event | category | flops | bytes accessed | tf_op | source)
XLA Modules:
  0.0 575.1 jit_solution(11662185768139078073)
XLA Ops:
  7.2 0.0 copy-start
  7.2 0.0 all-reduce.6.cloned.1.call-start
  7.2 1.5 copy-done
  8.8 28.9 %fusion.1 = f32[2,4096,256]{2,1,0:T(8,128)} fusion(bf16[2,4096,4096]{2,1,0:T(8,128)(2,1)} %param.2, bf16[4096,256]{1,0:T(8,128)(2,1)S(1)} %copy-done), kind=kOutput, calls=%fused_computation.4 | convolution fusion | flops 17179869184 | bytes 77594624 | tf_op jit(solution)/shard_map/mrd,dk->mrk/dot_general | solution.py:19
  37.6 149.1 %all-reduce.9 = bf16[2,4096,256]{2,1,0:T(8,128)(2,1)} all-reduce(f32[2,4096,256]{2,1,0:T(8,128)} %fusion.1), channel_id=1, replica_groups=mesh['row'=8,'col'=4] {'col'}, use_global_device_ids=true, to_apply=%region_0.0 | all-reduce | flops 2097152 | bytes 12582912 | tf_op jit(solution)/shard_map/psum | solution.py:22
  186.7 6.0 %fusion.18 = f32[2,256,256]{1,2,0:T(8,128)} fusion(bf16[2,4096,256]{2,1,0:T(8,128)(2,1)} %all-reduce.9), kind=kOutput, calls=%fused_computation.43 | convolution fusion | flops 1073741824 | bytes 4718592 | tf_op jit(solution)/shard_map/mrk,mrl->mkl/dot_general | solution.py:26
  192.7 0.0 all-reduce.6.cloned.1.call-update
  192.7 0.0 all-reduce.8.cloned.1.call-start
  192.8 0.6 iota_compare_fusion.2
  193.4 38.2 %fusion.19 = f32[2,256,4096]{1,2,0:T(8,128)} fusion(bf16[2,4096,256]{2,1,0:T(8,128)(2,1)} %all-reduce.9, bf16[2,4096,4096]{2,1,0:T(8,128)(2,1)} %param.2), kind=kOutput, calls=%fused_computation.44 | convolution fusion | flops 17179869184 | bytes 79691776 | tf_op jit(solution)/shard_map/mrk,mrd->mkd/dot_general | solution.py:35
  231.6 0.6 iota_multiply_fusion
  232.2 0.6 iota_compare_fusion.1
  232.8 0.7 fusion.17
  233.5 32.1 %all-reduce.6.cloned.1.call-done = f32[2,256,256]{1,2,0:T(8,128)} async-done(((f32[2,256,256]{1,2,0:T(8,128)}), f32[2,256,256]{1,2,0:T(8,128)}) %all-reduce.6.cloned.1.call-update) | async-done | bytes 524304 | tf_op jit(solution)/shard_map/psum | solution.py:29
  265.6 1.1 broadcast_multiply_fusion
  266.7 0.2 copy.24
  266.9 1.1 fusion.4
  268.0 0.0 copy-start.1
  268.0 0.8 copy-done.1
  268.8 23.5 %custom-call.17 = f32[2,128,128]{2,1,0:T(8,128)S(1)} custom-call(f32[2,128,128]{2,1,0:T(8,128)S(1)} %cholesky.122), custom_call_target="Cholesky" | custom-call | tf_op jit(solution)/shard_map/jit(cholesky)/cholesky | solution.py:30
  292.3 0.7 select_bitcast_fusion
  293.1 19.7 %custom-call.18 = f32[2,1,128,128]{2,3,1,0:T(8,128)S(1)} custom-call(f32[2,1,128,128]{3,2,1,0:T(8,128)S(1)} %select_bitcast_fusion), custom_call_target="InvertDiagBlocksLowerTriangular" | custom-call | tf_op jit(solution)/shard_map/jit(cholesky)/cholesky | solution.py:30
  312.8 1.2 constant_dynamic-update-slice_fusion.1
  313.9 1.3 convolution_subtract_fusion.1
  315.3 23.7 %custom-call.19 = f32[2,128,128]{2,1,0:T(8,128)S(1)} custom-call(f32[2,128,128]{2,1,0:T(8,128)S(1)} %convolution_subtract_fusion.1), custom_call_target="Cholesky" | custom-call | tf_op jit(solution)/shard_map/jit(cholesky)/cholesky | solution.py:30
  339.0 0.2 compare_reduce_fusion
  339.1 1.0 select_select_fusion
  340.1 0.7 triangular_solve.66
  340.9 5.1 while.1
  340.9 0.6 fusion.31
  341.4 2.0 bitcast_dynamic-update-slice_fusion.2
  343.4 0.6 fusion.31
  344.0 2.0 bitcast_dynamic-update-slice_fusion.2
  346.0 40.1 %custom-call.20 = f32[2,2,128,128]{2,3,1,0:T(8,128)S(1)} custom-call(f32[2,2,128,128]{3,2,1,0:T(8,128)} %bitcast.48), custom_call_target="InvertDiagBlocksLowerTriangular" | custom-call | tf_op jit(solution)/shard_map/vmap(jit(_solve_triangular))/triangular_solve | solution.py:11
  386.1 1.3 fusion.8
  387.5 0.4 convolution_subtract_fusion
  387.8 0.4 fusion.7
  388.3 10.5 %fusion = bf16[256,2,4096]{0,2,1:T(8,128)(2,1)} fusion(f32[2,256,4096]{1,2,0:T(8,128)} %fusion.19, f32[2,128,256]{2,1,0:T(8,128)S(1)} %fusion.7, f32[2,128,256]{2,1,0:T(8,128)S(1)} %fusion.8), kind=kOutput, calls=%fused_computation.3 | convolution fusion | flops 6446776320 | bytes 13107200 | tf_op jit(solution)/shard_map/mck,mkd->cmd/dot_general | solution.py:39
  398.8 11.3 %copy.32 = bf16[256,2,4096]{2,1,0:T(2,128)(2,1)} copy(bf16[256,2,4096]{0,2,1:T(8,128)(2,1)} %fusion) | data formatting | bytes 8388608 | tf_op jit(solution)/shard_map/convert_element_type | solution.py:41
  410.0 0.0 copy-start.2
  410.0 0.0 all-reduce.8.cloned.1.call-update
  410.1 0.6 copy-done.2
  410.7 0.6 dynamic-slice.4
  411.9 3.3 convolution_convert_fusion
  415.2 150.6 %all-reduce.8.cloned.1.call-done = bf16[256,2,4096]{2,1,0:T(2,128)(2,1)} async-done(((bf16[256,2,4096]{2,1,0:T(2,128)(2,1)}), bf16[256,2,4096]{2,1,0:T(2,128)(2,1)}) %all-reduce.8.cloned.1.call-update) | async-done | bytes 4194320
  565.8 2.4 dynamic-slice_convert_fusion
  (9 shorter events, 0.1 us)
Async XLA Ops:
  7.2 1.6 copy-start
  7.2 258.4 %all-reduce.6.cloned.1.call-start = ((), (), s32[]{:S(2)}) async-start(), calls=%async_computation | async-start | bytes 1048576 | tf_op jit(solution)/shard_map/psum | solution.py:29
  192.7 373.0 %all-reduce.8.cloned.1.call-start = ((), (), s32[]{:S(2)}) async-start(), calls=%async_computation.1 | async-start | bytes 8388608
  268.0 0.8 copy-start.1
  410.0 0.7 copy-start.2
Sparse Core Ops, SparseCore 0:
  192.9 72.7 all-reduce.5
  410.2 155.5 all-reduce.7
where the time goes:
time: 576 us; the launch traced here: 575 us
  waiting for transfers between devices  183 us (32%)
  blocking collectives  149 us (26%)
  other arithmetic  115 us (20%)
  matrix products  91.4 us (16%)
  local copies, waits for them, and re-layouts  21.6 us (4%)
  between operations  14.8 us (3%)
    unnamed x3, waiting for transfers between devices  151 us
    psum x1, blocking collectives, body(): summed = lax.psum(partial_sketch, 'col')  149 us
    another operation x9, other arithmetic, body(): factor_low = jnp.linalg.cholesky(gram_sum / total_rows)  68.4 us
    another operation x4, other arithmetic, invert_low(): jax.scipy.linalg.solve_triangular(matrix, identity, lower=True)  42.3 us
    dot_general x1, matrix products, body(): jnp.einsum('mrk,mrd->mkd', sketch_rows, gradients, preferred_element_type...  38.2 us
    psum x1, waiting for transfers between devices, body(): gram_sum = lax.psum(local_gram, 'row')  32.1 us
    dot_general x1, matrix products, body(): jnp.einsum('mrd,dk->mrk', gradients, sketch_matrix, preferred_element_typ...  28.9 us
  transfers between devices with their start and end apart: 2, of which 2 were waited for; matrix products, arithmetic and copies ran while one was open for 8% of the time, Pallas kernels for 0%

commit v1 on v0

v1 whole, which is shorter than its diff:
```python
import functools
import math

import jax
import jax.numpy as jnp
from jax import lax
from jax.experimental import pallas as pl
from jax.experimental.pallas import tpu as pltpu
from jax.sharding import PartitionSpec as P

HIGHEST = lax.Precision.HIGHEST


def factor_inverse_kernel(scale, block, gram_ref, inverse_ref, work):
    count, rank, _ = gram_ref.shape
    lanes = lax.broadcasted_iota(jnp.int32, (rank, rank), 1)
    rows = lax.broadcasted_iota(jnp.int32, (rank, rank), 0)
    for m in range(count):
        work[m, :, :rank] = gram_ref[m] * scale
        work[m, :, rank:] = jnp.where(lanes == rows, 1.0, 0.0).astype(jnp.float32)
    small_rows = lax.broadcasted_iota(jnp.int32, (block, 2 * block), 0)
    small_lanes = lax.broadcasted_iota(jnp.int32, (block, 2 * block), 1)
    identity = jnp.where(small_rows + block == small_lanes, 1.0, 0.0).astype(jnp.float32)[:, block:]
    for step in range(rank // block):
        low = step * block
        heads = [
            jnp.concatenate([work[m, low : low + block, low : low + block], identity], axis=1)
            for m in range(count)
        ]
        scales = [jnp.zeros((block, 2 * block), jnp.float32) for _ in range(count)]
        for j in range(block):
            for m in range(count):
                head = heads[m]
                column = jnp.broadcast_to(head[:, j : j + 1], head.shape)
                pivot = column[j : j + 1, :]
                row = head[j : j + 1, :]
                ratio = row / pivot
                heads[m] = head - jnp.where(small_rows > j, column, 0.0) * ratio
                scales[m] = jnp.where(small_rows == j, lax.rsqrt(pivot), scales[m])
        for m in range(count):
            corner = (heads[m] * scales[m])[:, block:]
            panel = jnp.dot(corner, work[m, low : low + block, :], precision=HIGHEST, preferred_element_type=jnp.float32)
            work[m, low : low + block, :] = panel
            if low + block < rank:
                work[m, low + block :, :] -= lax.dot_general(
                    panel[:, low + block : rank], panel, (((0,), (0,)), ((), ())),
                    precision=HIGHEST, preferred_element_type=jnp.float32,
                )
    for m in range(count):
        inverse_ref[m] = jnp.where(lanes <= rows, work[m, :, rank:], 0.0)


def factor_inverse(gram_sum, total_rows):
    count, rank, _ = gram_sum.shape
    return pl.pallas_call(
        functools.partial(factor_inverse_kernel, 1.0 / total_rows, 32),
        out_shape=jax.ShapeDtypeStruct(gram_sum.shape, jnp.float32),
        in_specs=[pl.BlockSpec(memory_space=pltpu.VMEM)],
        out_specs=pl.BlockSpec(memory_space=pltpu.VMEM),
        scratch_shapes=[pltpu.VMEM((count, rank, 2 * rank), jnp.float32)],
        compiler_params=pltpu.CompilerParams(vmem_limit_bytes=16 << 20),
        cost_estimate=pl.CostEstimate(flops=20_000_000_000, bytes_accessed=2 << 20, transcendentals=0),
    )(gram_sum)


MESH = pl.DeviceIdType.MESH
SLOTS = 7
BLOCK = 256
TILE = 1024


def remote(source, target, send_sem, recv_sem, device):
    return pltpu.make_async_remote_copy(
        src_ref=source, dst_ref=target, send_sem=send_sem, recv_sem=recv_sem,
        device_id=device, device_id_type=MESH,
    )


def range_kernel(
    which, omega_ref, grad_ref, own_ref, gram_ref, keep_ref, give_ref, ring, total, parts,
    send_core, recv_core, send_chip, recv_chip, sums, grad_sem, send_sems, recv_sems,
):
    blocks = sums.shape[0]
    half_rows, rank = sums.shape[2:]
    row, col = lax.axis_index("row"), lax.axis_index("col")
    core = lax.rem(col, 2)
    sibling = (row, col + 1 - 2 * core)
    across = (row, lax.rem(col + 2, 4))

    def fetch(b):
        return pltpu.make_async_copy(
            grad_ref.at[which, pl.ds(b * BLOCK, BLOCK), :], ring.at[lax.rem(b, SLOTS)],
            grad_sem.at[lax.rem(b, SLOTS)],
        )

    def copy_partial(b):
        return remote(send_core.at[b], recv_core.at[b], send_sems.at[0, b], recv_sems.at[0, b], sibling)

    def copy_chip(b):
        return remote(send_chip.at[b], recv_chip.at[b], send_sems.at[1, b], recv_sems.at[1, b], across)

    def copy_sum(b):
        return remote(sums.at[b, core], sums.at[b, core], send_sems.at[2, b], recv_sems.at[2, b], sibling)

    for b in range(SLOTS):
        fetch(b).start()
    barrier = pltpu.get_barrier_semaphore()
    for peer in (sibling, across):
        pl.semaphore_signal(barrier, inc=1, device_id=peer, device_id_type=MESH)
    total[...] = jnp.zeros_like(total)
    gram_ref[...] = jnp.zeros_like(gram_ref)
    pl.semaphore_wait(barrier, 2)

    def step(s, carry):
        @pl.when(s < blocks)
        def _():
            fetch(s).wait()
            partial = jnp.dot(ring[lax.rem(s, SLOTS)], omega_ref[...], preferred_element_type=jnp.float32)
            parts[lax.rem(s, 2)] = partial.reshape(2, half_rows, rank)
            send_core[s] = parts[lax.rem(s, 2), 1 - core].astype(jnp.bfloat16)
            copy_partial(s).start()

        @pl.when((s >= 1) & (s < blocks + 1))
        def _():
            b = s - 1
            copy_partial(b).wait_recv()
            send_chip[b] = (parts[lax.rem(b, 2), core] + recv_core[b].astype(jnp.float32)).astype(jnp.bfloat16)
            copy_chip(b).start()

        @pl.when((s >= 3) & (s < blocks + 3))
        def _():
            b = s - 3
            copy_chip(b).wait_recv()
            sums[b, core] = (send_chip[b].astype(jnp.float32) + recv_chip[b].astype(jnp.float32)).astype(jnp.bfloat16)
            copy_sum(b).start()

        @pl.when(s >= 4)
        def _():
            b = s - 4
            copy_sum(b).wait_recv()
            block = sums[b].reshape(BLOCK, rank)
            turned = block.astype(jnp.float32).T.astype(jnp.bfloat16)
            gram_ref[...] += jnp.dot(turned, block, preferred_element_type=jnp.float32)
            slot = lax.rem(b, SLOTS)
            for low in range(0, total.shape[1], TILE):
                total[:, low : low + TILE] += jnp.dot(
                    turned, ring[slot, :, low : low + TILE], preferred_element_type=jnp.float32
                )

            @pl.when(b + SLOTS < blocks)
            def _():
                fetch(b + SLOTS).start()

        return carry

    lax.fori_loop(0, blocks + 4, step, 0)
    pairs, _, share = keep_ref.shape
    low = lax.rem(row, 2)
    for k in range(pairs):
        pair = 2 * lax.rem(row // 2 + k, pairs)
        keep_ref[k] = total[:, pl.ds(pl.multiple_of((pair + low) * share, share), share)].astype(jnp.bfloat16)
        give_ref[k] = total[:, pl.ds(pl.multiple_of((pair + 1 - low) * share, share), share)].astype(jnp.bfloat16)
    own = own_ref.shape[0]
    for i in range(own):
        own_ref[i] = sums[col * own + i].reshape(BLOCK, rank)

    def finish(b, carry):
        copy_partial(b).wait_send()
        copy_chip(b).wait_send()
        copy_sum(b).wait_send()
        return carry

    lax.fori_loop(0, blocks, finish, 0)


def sketch_and_moment(which, gradients, sketch_matrix, devices):
    _, rows, width = gradients.shape
    rank = sketch_matrix.shape[1]
    blocks = rows // BLOCK
    half = (blocks, BLOCK // 2, rank)
    vmem = pl.BlockSpec(memory_space=pltpu.VMEM)
    moment_half = jax.ShapeDtypeStruct((devices // 2, rank, width // devices), jnp.bfloat16)
    own, gram, keep, give = pl.pallas_call(
        functools.partial(range_kernel, which),
        out_shape=(
            jax.ShapeDtypeStruct((blocks // 4, BLOCK, rank), jnp.bfloat16),
            jax.ShapeDtypeStruct((rank, rank), jnp.float32),
            moment_half,
            moment_half,
        ),
        in_specs=[vmem, pl.BlockSpec(memory_space=pl.ANY)],
        out_specs=(vmem, vmem, vmem, vmem),
        scratch_shapes=[
            pltpu.VMEM((SLOTS, BLOCK, width), jnp.bfloat16),
            pltpu.VMEM((rank, width), jnp.float32),
            pltpu.VMEM((2, 2, BLOCK // 2, rank), jnp.float32),
            pltpu.VMEM(half, jnp.bfloat16),
            pltpu.VMEM(half, jnp.bfloat16),
            pltpu.VMEM(half, jnp.bfloat16),
            pltpu.VMEM(half, jnp.bfloat16),
            pltpu.VMEM((blocks, 2, BLOCK // 2, rank), jnp.bfloat16),
            pltpu.SemaphoreType.DMA((SLOTS,)),
            pltpu.SemaphoreType.DMA((3, blocks)),
            pltpu.SemaphoreType.DMA((3, blocks)),
        ],
        compiler_params=pltpu.CompilerParams(
            collective_id=which, has_side_effects=True, vmem_limit_bytes=44 << 20
        ),
        cost_estimate=pl.CostEstimate(
            flops=4 * rows * width * rank, bytes_accessed=2 * rows * width, transcendentals=0
        ),
    )(sketch_matrix, gradients)
    return own.reshape(rows // 4, rank), gram, keep, give


def gram_kernel(gram_ref, sum_ref, landed, row_send, row_recv, out_send, out_recv, col_send, col_recv):
    count, piece, _ = landed.shape
    row, col = lax.axis_index("row"), lax.axis_index("col")
    cols = lax.axis_size("col")
    quarter = count * piece
    base = col * quarter
    rows_of = lambda r: pl.ds(pl.multiple_of(base + r * piece, piece), piece)
    row_peers = [(lax.rem(row + k, count), col) for k in range(1, count)]
    col_peers = [(row, lax.rem(col + k, cols)) for k in range(1, cols)]
    barrier = pltpu.get_barrier_semaphore()
    for peer in row_peers + col_peers:
        pl.semaphore_signal(barrier, inc=1, device_id=peer, device_id_type=MESH)
    pl.semaphore_wait(barrier, count + cols - 2)

    first = [
        remote(gram_ref.at[rows_of(peer[0])], landed.at[k], row_send.at[k], row_recv.at[k], peer)
        for k, peer in enumerate(row_peers)
    ]
    for copy in first:
        copy.start()
    here = gram_ref[rows_of(row)]
    for k, copy in enumerate(first):
        copy.wait_recv()
        here += landed[k]
    sum_ref[rows_of(row)] = here
    second = [
        remote(sum_ref.at[rows_of(row)], sum_ref.at[rows_of(row)], out_send.at[k], out_recv.at[k], peer)
        for k, peer in enumerate(row_peers)
    ]
    for copy in second:
        copy.start()
    for copy in second:
        copy.wait_recv()
    mine = pl.ds(pl.multiple_of(base, quarter), quarter)
    third = [
        remote(sum_ref.at[mine], sum_ref.at[mine], col_send.at[k], col_recv.at[k], peer)
        for k, peer in enumerate(col_peers)
    ]
    for copy in third:
        copy.start()
    for copy in third:
        copy.wait_recv()
    for copy in first + second + third:
        copy.wait_send()


def add_grams(gram, rows, cols):
    lines, rank = gram.shape
    piece = lines // (rows * cols)
    vmem = pl.BlockSpec(memory_space=pltpu.VMEM)
    return pl.pallas_call(
        gram_kernel,
        out_shape=jax.ShapeDtypeStruct(gram.shape, jnp.float32),
        in_specs=[vmem],
        out_specs=vmem,
        scratch_shapes=[pltpu.VMEM((rows, piece, rank), jnp.float32)]
        + [pltpu.SemaphoreType.DMA((rows - 1,))] * 4
        + [pltpu.SemaphoreType.DMA((cols - 1,))] * 2,
        compiler_params=pltpu.CompilerParams(
            collective_id=2, has_side_effects=True, vmem_limit_bytes=8 << 20
        ),
        cost_estimate=pl.CostEstimate(flops=20_000_000_000, bytes_accessed=2 << 20, transcendentals=0),
    )(gram)


def finish_outputs(mine, gram_sum, moments, total_rows):
    inverse_low = factor_inverse(gram_sum, total_rows)
    inverse_low, moments = lax.optimization_barrier((inverse_low, moments))
    projector = jnp.einsum(
        "mrk,mlk->mrl", mine.astype(jnp.float32), inverse_low, precision=HIGHEST
    ).astype(jnp.bfloat16)
    scaled = inverse_low * (1.0 / math.sqrt(total_rows))
    part = jnp.stack(
        [jnp.dot(scaled[m], moments[m].astype(jnp.float32), precision=HIGHEST) for m in range(2)], 1
    ).astype(jnp.bfloat16)
    projected = lax.all_to_all(part, "row", split_axis=0, concat_axis=2, tiled=True).astype(jnp.float32)
    return (projector, projected)


def add_pairs(keep, give, devices):
    got = lax.ppermute(give, "row", [(r, r + 1 - 2 * (r % 2)) for r in range(devices)])
    paired = keep.astype(jnp.float32) + got.astype(jnp.float32)
    return paired[0], [paired[k].astype(jnp.bfloat16) for k in range(1, devices // 2)]


def add_moments(first, others, devices):
    moment = first
    for k, other in enumerate(others, 1):
        ring = [(r, (r + 2 * k) % devices) for r in range(devices)]
        moment += lax.ppermute(other, "row", ring).astype(jnp.float32)
    return moment


def body_fused(gradients, sketch_matrix):
    rows, cols = lax.axis_size("row"), lax.axis_size("col")
    mine, grams, pairs = [], [], []
    for m in range(2):
        own, gram, keep, give = sketch_and_moment(m, gradients, sketch_matrix, rows)
        mine.append(own)
        grams.append(gram)
        pairs.append(add_pairs(keep, give, rows))
    rank = sketch_matrix.shape[1]
    grams, pairs[0] = lax.optimization_barrier((grams, pairs[0]))
    moment = add_moments(*pairs[0], rows)
    gram_sum = add_grams(jnp.concatenate(grams, 0), rows, cols)
    gram_sum, moment, pairs[1] = lax.optimization_barrier((gram_sum, moment, pairs[1]))
    moments = [moment, add_moments(*pairs[1], rows)]
    return finish_outputs(jnp.stack(mine), gram_sum.reshape(2, rank, rank), moments, gradients.shape[1] * rows)


def body_plain(gradients, sketch_matrix):
    total_rows = gradients.shape[1] * lax.axis_size("row")
    partial_sketch = jnp.einsum(
        "mrd,dk->mrk", gradients, sketch_matrix, preferred_element_type=jnp.float32
    ).astype(jnp.bfloat16)
    mine = lax.psum_scatter(partial_sketch, "col", scatter_dimension=1, tiled=True)
    sketch_rows = lax.all_gather(mine, "col", axis=1, tiled=True)
    local_gram = jnp.einsum("mrk,mrl->mkl", mine, mine, preferred_element_type=jnp.float32)
    gram_sum = lax.psum(local_gram, ("row", "col"))
    moments = []
    for m in range(2):
        moment = jnp.einsum("rk,rd->kd", sketch_rows[m], gradients[m], preferred_element_type=jnp.float32)
        moments.append(lax.psum_scatter(moment.astype(jnp.bfloat16), "row", scatter_dimension=1, tiled=True))
    return finish_outputs(mine, gram_sum, moments, total_rows)


def solution(mesh):
    in_specs = (P(None, "row", "col"), P("col", None))
    out_specs = (P(None, ("row", "col"), None), P("row", None, "col"))

    def body(gradients, sketch_matrix):
        _, rows, width = gradients.shape
        rank = sketch_matrix.shape[1]
        fits = mesh.shape["col"] == 4 and mesh.shape["row"] % 2 == 0 and rows % (4 * BLOCK) == 0 and rows >= SLOTS * BLOCK and width % TILE == 0 and width % (128 * mesh.shape["row"]) == 0
        fits = fits and (2 * rank) % (16 * mesh.shape["row"] * mesh.shape["col"]) == 0
        return (body_fused if fits else body_plain)(gradients, sketch_matrix)

    return jax.shard_map(body, mesh=mesh, in_specs=in_specs, out_specs=out_specs, check_vma=False)
```

time: 576 us -> 173 us (0.30)
  waiting for transfers between devices: 183 us -> 13.2 us
  blocking collectives: 149 us -> 0 us
  Pallas kernels: 0 us -> 133 us
  other arithmetic: 115 us -> 1.57 us
  matrix products: 91.4 us -> 3.25 us
  local copies, waits for them, and re-layouts: 21.6 us -> 4.66 us
  starting transfers between devices: 0.08 us -> 15.9 us
  between operations: 14.8 us -> 0.84 us
    unnamed x3 -> x0, waiting for transfers between devices: 151 us -> none
    psum x1 -> x0, blocking collectives: 149 us -> none  [body(): summed = lax.psum(partial_sketch, 'col')]
    pallas_call x0 -> x4, Pallas kernels: none -> 133 us  [the longest x2 70.2 us: sketch_and_moment(): pl.pallas_call(functools.partial(range_kernel, which), out_shape=(jax.Sha...]
    another operation x13 -> x3, other arithmetic: 111 us -> 0.86 us  [the longest x9 68.4 us: body(): factor_low = jnp.linalg.cholesky(gram_sum / total_rows)]
    dot_general x5 -> x3, matrix products: 86.8 us -> 3.25 us  [the longest x1 2.02 us: finish_outputs(): jnp.einsum('mrk,mlk->mrl', mine.astype(jnp.float32), inverse_low, precisi...]
    psum x1 -> x0, waiting for transfers between devices: 32.1 us -> none  [body(): gram_sum = lax.psum(local_gram, 'row')]
    all_to_all x0 -> x1, waiting for transfers between devices: none -> 13.2 us  [finish_outputs(): lax.all_to_all(part, 'row', split_axis=0, concat_axis=2, tiled=True)]
    ppermute x0 -> x8, starting transfers between devices: none -> 12.5 us  [the longest x6 10.3 us: add_moments(): moment += lax.ppermute(other, 'row', ring).astype(jnp.float32)]
  transfers between devices with their start and end apart: 2 -> 9, of which waited for: 2 -> 1; matrix products, arithmetic and copies ran while one was open for 8% -> 2% of each run, Pallas kernels for 0% -> 56%
where the time goes in v1:
time: 173 us
  Pallas kernels  133 us (77%)
  starting transfers between devices  15.9 us (9%)
  waiting for transfers between devices  13.2 us (8%)
  local copies, waits for them, and re-layouts  4.66 us (3%)
  matrix products  3.25 us (2%)
    pallas_call x2, Pallas kernels, sketch_and_moment(): pl.pallas_call(functools.partial(range_kernel, which), out_shape=(jax.Sha...  70.2 us
    pallas_call x1, Pallas kernels, add_grams(): pl.pallas_call(gram_kernel, out_shape=jax.ShapeDtypeStruct(gram.shape, jn...  33.8 us
    pallas_call x1, Pallas kernels, factor_inverse(): pl.pallas_call(functools.partial(factor_inverse_kernel, 1.0 / total_rows,...  29.4 us
    all_to_all x1, waiting for transfers between devices, finish_outputs(): lax.all_to_all(part, 'row', split_axis=0, concat_axis=2, tiled=True)  13.2 us
    ppermute x6, starting transfers between devices, add_moments(): moment += lax.ppermute(other, 'row', ring).astype(jnp.float32)  10.3 us
    all_to_all x1, starting transfers between devices, finish_outputs(): lax.all_to_all(part, 'row', split_axis=0, concat_axis=2, tiled=True)  3.49 us
  transfers between devices with their start and end apart: 9, of which 1 were waited for; matrix products, arithmetic and copies ran while one was open for 2% of the time, Pallas kernels for 56%

profile of v1, /device:TPU:0, one launch (start us, length us, event | category | flops | bytes accessed | tf_op | source)
XLA Modules:
  0.0 172.8 jit_solution(7700406852898906159)
XLA Ops:
  0.6 0.0 copy-start
  0.6 1.6 copy-done
  2.2 36.1 %shard_map.41 = (bf16[4,256,256]{2,1,0:T(8,128)(2,1)S(1)}, f32[256,256]{1,0:T(8,128)S(1)}, bf16[4,256,512]{2,1,0:T(8,128)(2,1)S(1)}, bf16[4,256,512]{2,1,0:T(8,128)(2,1)S(1)}) custom-call(bf16[4096,256]{1,0:T(8,128)(2,1)S(1)} %copy-done, bf16[2,4096,4096]{2,1,0:T(8,128)(2,1)} %grad_ref.3), custom_call_target="tpu_custom_call" | custom-call | flops 17179869184 | bytes 33554432 | tf_op jit(solution)/shard_map/pallas_call | solution.py:183
  38.3 1.6 collective-permute-start
  39.9 34.1 %shard_map.42 = (bf16[4,256,256]{2,1,0:T(8,128)(2,1)S(1)}, f32[256,256]{1,0:T(8,128)S(1)}, bf16[4,256,512]{2,1,0:T(8,128)(2,1)S(1)}, bf16[4,256,512]{2,1,0:T(8,128)(2,1)S(1)}) custom-call(bf16[4096,256]{1,0:T(8,128)(2,1)S(1)} %copy-done, bf16[2,4096,4096]{2,1,0:T(8,128)(2,1)} %grad_ref.3), custom_call_target="tpu_custom_call" | custom-call | flops 17179869184 | bytes 33554432 | tf_op jit(solution)/shard_map/pallas_call | solution.py:183
  74.0 0.6 collective-permute-start.4
  74.6 0.0 collective-permute-done
  74.6 0.4 fusion.6
  75.0 0.1 slice_bitcast_fusion.9
  75.1 1.6 collective-permute-start.1
  76.7 2.6 %collective-permute-start.2 = (bf16[256,512]{1,0:T(8,128)(2,1)S(1)}, bf16[256,512]{1,0:T(8,128)(2,1)S(1)}, u32[]{:S(2)}, u32[]{:S(2)}) collective-permute-start(bf16[256,512]{1,0:T(8,128)(2,1)S(1)} %get-tuple-element.35), channel_id=1, source_target_pairs={{0,16},{4,20},{8,24},{12,28},{16,0},{20,4},{24,8},{28,12},{1,17},{... | collective-permute-start | bytes 786440 | tf_op jit(solution)/shard_map/ppermute | solution.py:305
  79.3 1.3 collective-permute-start.3
  80.7 33.8 %shard_map.43 = f32[512,256]{1,0:T(8,128)S(1)} custom-call(f32[512,256]{1,0:T(8,128)S(1)} %pad_maximum_fusion.gram_ref), custom_call_target="tpu_custom_call" | custom-call | flops 20000000000 | bytes 2097152 | tf_op jit(solution)/shard_map/pallas_call | solution.py:266
  114.5 0.0 collective-permute-done.4
  114.5 0.4 fusion.7
  114.9 0.1 slice_bitcast_fusion.6
  115.0 0.0 collective-permute-done.1
  115.0 0.0 collective-permute-done.2
  115.0 0.0 collective-permute-done.3
  115.1 0.1 convert_add_fusion.3
  115.2 0.9 collective-permute-start.5
  116.1 2.7 %collective-permute-start.6 = (bf16[256,512]{1,0:T(8,128)(2,1)S(1)}, bf16[256,512]{1,0:T(8,128)(2,1)S(1)}, u32[]{:S(2)}, u32[]{:S(2)}) collective-permute-start(bf16[256,512]{1,0:T(8,128)(2,1)S(1)} %get-tuple-element.43), channel_id=1, source_target_pairs={{0,16},{4,20},{8,24},{12,28},{16,0},{20,4},{24,8},{28,12},{1,17},{... | collective-permute-start | bytes 786440 | tf_op jit(solution)/shard_map/ppermute | solution.py:305
  118.9 1.1 collective-permute-start.7
  119.9 29.4 %shard_map.44 = f32[2,256,256]{2,1,0:T(8,128)S(1)} custom-call(f32[2,256,256]{2,1,0:T(8,128)S(1)} %bitcast.40), custom_call_target="tpu_custom_call" | custom-call | flops 20000000000 | bytes 2097152 | tf_op jit(solution)/shard_map/pallas_call | solution.py:55
  149.3 0.0 collective-permute-done.5
  149.3 0.0 collective-permute-done.6
  149.3 0.0 collective-permute-done.7
  149.3 0.1 convert_add_fusion.2
  149.5 0.6 fusion
  150.1 0.6 fusion.1
  150.8 0.1 pad_maximum_fusion.1
  150.8 1.3 copy.5
  152.2 3.5 %all-to-all-start = ((bf16[256,2,512]{2,1,0:T(2,128)(2,1)}), bf16[256,2,512]{2,1,0:T(2,128)(2,1)S(1)}, u32[]{:S(2)}, u32[]{:S(2)}) async-start(bf16[256,2,512]{2,1,0:T(2,128)(2,1)} %copy.5), calls=%async_computation | async-start | bytes 1048576 | tf_op jit(solution)/shard_map/all_to_all | solution.py:291
  155.7 2.0 %convolution_convert_fusion = bf16[2,1024,256]{2,1,0:T(8,128)(2,1)} fusion(f32[2,256,256]{2,1,0:T(8,128)S(1)} %shard_map.44, bf16[1,1024,256]{2,1,0:T(8,128)(2,1)S(1)} %bitcast.39, bf16[1,1024,256]{2,1,0:T(8,128)(2,1)S(1)} %bitcast.38), kind=kOutput, calls=%fused_computation.2 | convolution fusion | flops 1611661312 | bytes 2621440 | tf_op jit(solution)/shard_map/mrk,mlk->mrl/dot_general | solution.py:284
  157.7 13.2 %all-to-all-done = bf16[256,2,512]{2,1,0:T(2,128)(2,1)S(1)} async-done(((bf16[256,2,512]{2,1,0:T(2,128)(2,1)}), bf16[256,2,512]{2,1,0:T(2,128)(2,1)S(1)}, u32[]{:S(2)}, u32[]{:S(2)}) %all-to-all-start) | async-done | bytes 524320 | tf_op jit(solution)/shard_map/all_to_all | solution.py:291
  170.9 0.4 convert_bitcast_fusion
  171.3 1.6 copy.7
  (4 shorter events, 0.2 us)
Async XLA Ops:
  0.6 1.6 copy-start
  38.3 36.2 %collective-permute-start = (bf16[4,256,512]{2,1,0:T(8,128)(2,1)S(1)}, bf16[4,256,512]{2,1,0:T(8,128)(2,1)S(1)}, u32[]{:S(2)}, u32[]{:S(2)}) collective-permute-start(bf16[4,256,512]{2,1,0:T(8,128)(2,1)S(1)} %get-tuple-element.30), channel_id=1, source_target_pairs={{0,4},{4,0},{8,12},{12,8},{16,20},{20,16},{24,28},{28,24},{1,5},{5... | collective-permute-start | bytes 3145736 | tf_op jit(solution)/shard_map/ppermute | solution.py:296
  74.0 40.5 %collective-permute-start.4 = (bf16[4,256,512]{2,1,0:T(8,128)(2,1)S(1)}, bf16[4,256,512]{2,1,0:T(8,128)(2,1)S(1)}, u32[]{:S(2)}, u32[]{:S(2)}) collective-permute-start(bf16[4,256,512]{2,1,0:T(8,128)(2,1)S(1)} %get-tuple-element.38), channel_id=1, source_target_pairs={{0,4},{4,0},{8,12},{12,8},{16,20},{20,16},{24,28},{28,24},{1,5},{5... | collective-permute-start | bytes 3145736 | tf_op jit(solution)/shard_map/ppermute | solution.py:296
  75.1 39.9 %collective-permute-start.1 = (bf16[256,512]{1,0:T(8,128)(2,1)S(1)}, bf16[256,512]{1,0:T(8,128)(2,1)S(1)}, u32[]{:S(2)}, u32[]{:S(2)}) collective-permute-start(bf16[256,512]{1,0:T(8,128)(2,1)S(1)} %get-tuple-element.34), channel_id=1, source_target_pairs={{0,8},{4,12},{8,16},{12,20},{16,24},{20,28},{24,0},{28,4},{1,9},{5... | collective-permute-start | bytes 786440 | tf_op jit(solution)/shard_map/ppermute | solution.py:305
  76.7 38.3 %collective-permute-start.2 = (bf16[256,512]{1,0:T(8,128)(2,1)S(1)}, bf16[256,512]{1,0:T(8,128)(2,1)S(1)}, u32[]{:S(2)}, u32[]{:S(2)}) collective-permute-start(bf16[256,512]{1,0:T(8,128)(2,1)S(1)} %get-tuple-element.35), channel_id=1, source_target_pairs={{0,16},{4,20},{8,24},{12,28},{16,0},{20,4},{24,8},{28,12},{1,17},{... | collective-permute-start | bytes 786440 | tf_op jit(solution)/shard_map/ppermute | solution.py:305
  79.3 35.7 %collective-permute-start.3 = (bf16[256,512]{1,0:T(8,128)(2,1)S(1)}, bf16[256,512]{1,0:T(8,128)(2,1)S(1)}, u32[]{:S(2)}, u32[]{:S(2)}) collective-permute-start(bf16[256,512]{1,0:T(8,128)(2,1)S(1)} %get-tuple-element.36), channel_id=1, source_target_pairs={{0,24},{4,28},{8,0},{12,4},{16,8},{20,12},{24,16},{28,20},{1,25},{... | collective-permute-start | bytes 786440 | tf_op jit(solution)/shard_map/ppermute | solution.py:305
  115.2 34.1 %collective-permute-start.5 = (bf16[256,512]{1,0:T(8,128)(2,1)S(1)}, bf16[256,512]{1,0:T(8,128)(2,1)S(1)}, u32[]{:S(2)}, u32[]{:S(2)}) collective-permute-start(bf16[256,512]{1,0:T(8,128)(2,1)S(1)} %get-tuple-element.42), channel_id=1, source_target_pairs={{0,8},{4,12},{8,16},{12,20},{16,24},{20,28},{24,0},{28,4},{1,9},{5... | collective-permute-start | bytes 786440 | tf_op jit(solution)/shard_map/ppermute | solution.py:305
  116.1 33.2 %collective-permute-start.6 = (bf16[256,512]{1,0:T(8,128)(2,1)S(1)}, bf16[256,512]{1,0:T(8,128)(2,1)S(1)}, u32[]{:S(2)}, u32[]{:S(2)}) collective-permute-start(bf16[256,512]{1,0:T(8,128)(2,1)S(1)} %get-tuple-element.43), channel_id=1, source_target_pairs={{0,16},{4,20},{8,24},{12,28},{16,0},{20,4},{24,8},{28,12},{1,17},{... | collective-permute-start | bytes 786440 | tf_op jit(solution)/shard_map/ppermute | solution.py:305
  118.9 30.5 %collective-permute-start.7 = (bf16[256,512]{1,0:T(8,128)(2,1)S(1)}, bf16[256,512]{1,0:T(8,128)(2,1)S(1)}, u32[]{:S(2)}, u32[]{:S(2)}) collective-permute-start(bf16[256,512]{1,0:T(8,128)(2,1)S(1)} %get-tuple-element.44), channel_id=1, source_target_pairs={{0,24},{4,28},{8,0},{12,4},{16,8},{20,12},{24,16},{28,20},{1,25},{... | collective-permute-start | bytes 786440 | tf_op jit(solution)/shard_map/ppermute | solution.py:305
  152.2 18.7 %all-to-all-start = ((bf16[256,2,512]{2,1,0:T(2,128)(2,1)}), bf16[256,2,512]{2,1,0:T(2,128)(2,1)S(1)}, u32[]{:S(2)}, u32[]{:S(2)}) async-start(bf16[256,2,512]{2,1,0:T(2,128)(2,1)} %copy.5), calls=%async_computation | async-start | bytes 1048576 | tf_op jit(solution)/shard_map/all_to_all | solution.py:291

commit v2 on v1

--- a/solution.py
+++ b/solution.py
@@ -28,15 +28,23 @@
             for m in range(count)
         ]
         scales = [jnp.zeros((block, 2 * block), jnp.float32) for _ in range(count)]
-        for j in range(block):
+        for j in range(0, block, 2):
             for m in range(count):
                 head = heads[m]
-                column = jnp.broadcast_to(head[:, j : j + 1], head.shape)
-                pivot = column[j : j + 1, :]
-                row = head[j : j + 1, :]
-                ratio = row / pivot
-                heads[m] = head - jnp.where(small_rows > j, column, 0.0) * ratio
+                left = jnp.broadcast_to(head[:, j : j + 1], head.shape)
+                right = jnp.broadcast_to(head[:, j + 1 : j + 2], head.shape)
+                pivot, cross = left[j : j + 1, :], left[j + 1 : j + 2, :]
+                ratio = cross / pivot
+                upper = head[j : j + 1, :] / pivot
+                lower = head[j + 1 : j + 2, :] - ratio * head[j : j + 1, :]
+                right = right - left * ratio
+                second = right[j + 1 : j + 2, :]
+                heads[m] = (
+                    head - jnp.where(small_rows > j, left, 0.0) * upper
+                    - jnp.where(small_rows > j + 1, right, 0.0) * (lower / second)
+                )
                 scales[m] = jnp.where(small_rows == j, lax.rsqrt(pivot), scales[m])
+                scales[m] = jnp.where(small_rows == j + 1, lax.rsqrt(second), scales[m])
         for m in range(count):
             corner = (heads[m] * scales[m])[:, block:]
             panel = jnp.dot(corner, work[m, low : low + block, :], precision=HIGHEST, preferred_element_type=jnp.float32)

time: 173 us -> 165 us (0.954)
  Pallas kernels: 133 us -> 125 us
    pallas_call x1, Pallas kernels: 29.4 us -> 20.7 us  [factor_inverse(): pl.pallas_call(functools.partial(factor_inverse_kernel, 1.0 / total_rows,...]
  transfers between devices with their start and end apart: 9 -> 9, of which waited for: 1 -> 1; matrix products, arithmetic and copies ran while one was open for 2% -> 2% of each run, Pallas kernels for 56% -> 54%
where the time goes in v2:
time: 165 us
  Pallas kernels  125 us (76%)
  starting transfers between devices  17.5 us (11%)
  waiting for transfers between devices  12.8 us (8%)
  local copies, waits for them, and re-layouts  4.66 us (3%)
  matrix products  3.25 us (2%)
    pallas_call x2, Pallas kernels, sketch_and_moment(): pl.pallas_call(functools.partial(range_kernel, which), out_shape=(jax.Sha...  70.2 us
    pallas_call x1, Pallas kernels, add_grams(): pl.pallas_call(gram_kernel, out_shape=jax.ShapeDtypeStruct(gram.shape, jn...  33.8 us
    pallas_call x1, Pallas kernels, factor_inverse(): pl.pallas_call(functools.partial(factor_inverse_kernel, 1.0 / total_rows,...  20.7 us
    all_to_all x1, waiting for transfers between devices, finish_outputs(): lax.all_to_all(part, 'row', split_axis=0, concat_axis=2, tiled=True)  12.7 us
    ppermute x6, starting transfers between devices, add_moments(): moment += lax.ppermute(other, 'row', ring).astype(jnp.float32)  10.3 us
    all_to_all x1, starting transfers between devices, finish_outputs(): lax.all_to_all(part, 'row', split_axis=0, concat_axis=2, tiled=True)  5.01 us
  transfers between devices with their start and end apart: 9, of which 1 were waited for; matrix products, arithmetic and copies ran while one was open for 2% of the time, Pallas kernels for 54%

profile of v2, /device:TPU:0, one launch (start us, length us, event | category | flops | bytes accessed | tf_op | source)
XLA Modules:
  0.0 165.2 jit_solution(9004836562395821908)
XLA Ops:
  0.6 0.0 copy-start
  0.6 1.6 copy-done
  2.2 36.1 %shard_map.41 = (bf16[4,256,256]{2,1,0:T(8,128)(2,1)S(1)}, f32[256,256]{1,0:T(8,128)S(1)}, bf16[4,256,512]{2,1,0:T(8,128)(2,1)S(1)}, bf16[4,256,512]{2,1,0:T(8,128)(2,1)S(1)}) custom-call(bf16[4096,256]{1,0:T(8,128)(2,1)S(1)} %copy-done, bf16[2,4096,4096]{2,1,0:T(8,128)(2,1)} %grad_ref.3), custom_call_target="tpu_custom_call" | custom-call | flops 17179869184 | bytes 33554432 | tf_op jit(solution)/shard_map/pallas_call | solution.py:191
  38.3 1.6 collective-permute-start
  39.9 34.1 %shard_map.42 = (bf16[4,256,256]{2,1,0:T(8,128)(2,1)S(1)}, f32[256,256]{1,0:T(8,128)S(1)}, bf16[4,256,512]{2,1,0:T(8,128)(2,1)S(1)}, bf16[4,256,512]{2,1,0:T(8,128)(2,1)S(1)}) custom-call(bf16[4096,256]{1,0:T(8,128)(2,1)S(1)} %copy-done, bf16[2,4096,4096]{2,1,0:T(8,128)(2,1)} %grad_ref.3), custom_call_target="tpu_custom_call" | custom-call | flops 17179869184 | bytes 33554432 | tf_op jit(solution)/shard_map/pallas_call | solution.py:191
  74.0 0.6 collective-permute-start.4
  74.6 0.0 collective-permute-done
  74.6 0.4 fusion.6
  75.0 0.1 slice_bitcast_fusion.9
  75.1 1.6 collective-permute-start.1
  76.7 2.6 %collective-permute-start.2 = (bf16[256,512]{1,0:T(8,128)(2,1)S(1)}, bf16[256,512]{1,0:T(8,128)(2,1)S(1)}, u32[]{:S(2)}, u32[]{:S(2)}) collective-permute-start(bf16[256,512]{1,0:T(8,128)(2,1)S(1)} %get-tuple-element.35), channel_id=1, source_target_pairs={{0,16},{4,20},{8,24},{12,28},{16,0},{20,4},{24,8},{28,12},{1,17},{... | collective-permute-start | bytes 786440 | tf_op jit(solution)/shard_map/ppermute | solution.py:313
  79.3 1.3 collective-permute-start.3
  80.7 33.8 %shard_map.43 = f32[512,256]{1,0:T(8,128)S(1)} custom-call(f32[512,256]{1,0:T(8,128)S(1)} %pad_maximum_fusion.gram_ref), custom_call_target="tpu_custom_call" | custom-call | flops 20000000000 | bytes 2097152 | tf_op jit(solution)/shard_map/pallas_call | solution.py:274
  114.5 0.0 collective-permute-done.4
  114.5 0.4 fusion.7
  114.9 0.1 slice_bitcast_fusion.6
  115.0 0.0 collective-permute-done.1
  115.0 0.0 collective-permute-done.2
  115.0 0.0 collective-permute-done.3
  115.1 0.1 convert_add_fusion.3
  115.2 0.9 collective-permute-start.5
  116.1 2.7 %collective-permute-start.6 = (bf16[256,512]{1,0:T(8,128)(2,1)S(1)}, bf16[256,512]{1,0:T(8,128)(2,1)S(1)}, u32[]{:S(2)}, u32[]{:S(2)}) collective-permute-start(bf16[256,512]{1,0:T(8,128)(2,1)S(1)} %get-tuple-element.43), channel_id=1, source_target_pairs={{0,16},{4,20},{8,24},{12,28},{16,0},{20,4},{24,8},{28,12},{1,17},{... | collective-permute-start | bytes 786440 | tf_op jit(solution)/shard_map/ppermute | solution.py:313
  118.9 1.1 collective-permute-start.7
  119.9 20.7 %shard_map.44 = f32[2,256,256]{2,1,0:T(8,128)S(1)} custom-call(f32[2,256,256]{2,1,0:T(8,128)S(1)} %bitcast.40), custom_call_target="tpu_custom_call" | custom-call | flops 20000000000 | bytes 2097152 | tf_op jit(solution)/shard_map/pallas_call | solution.py:63
  140.6 0.0 collective-permute-done.5
  140.6 0.0 collective-permute-done.6
  140.7 0.0 collective-permute-done.7
  140.7 0.1 convert_add_fusion.2
  140.9 0.6 fusion
  141.5 0.6 fusion.1
  142.1 0.1 pad_maximum_fusion.1
  142.2 1.3 copy.5
  143.5 5.0 %all-to-all-start = ((bf16[256,2,512]{2,1,0:T(2,128)(2,1)}), bf16[256,2,512]{2,1,0:T(2,128)(2,1)S(1)}, u32[]{:S(2)}, u32[]{:S(2)}) async-start(bf16[256,2,512]{2,1,0:T(2,128)(2,1)} %copy.5), calls=%async_computation | async-start | bytes 1048576 | tf_op jit(solution)/shard_map/all_to_all | solution.py:299
  148.5 2.0 %convolution_convert_fusion = bf16[2,1024,256]{2,1,0:T(8,128)(2,1)} fusion(f32[2,256,256]{2,1,0:T(8,128)S(1)} %shard_map.44, bf16[1,1024,256]{2,1,0:T(8,128)(2,1)S(1)} %bitcast.39, bf16[1,1024,256]{2,1,0:T(8,128)(2,1)S(1)} %bitcast.38), kind=kOutput, calls=%fused_computation.2 | convolution fusion | flops 1611661312 | bytes 2621440 | tf_op jit(solution)/shard_map/mrk,mlk->mrl/dot_general | solution.py:292
  150.5 12.7 %all-to-all-done = bf16[256,2,512]{2,1,0:T(2,128)(2,1)S(1)} async-done(((bf16[256,2,512]{2,1,0:T(2,128)(2,1)}), bf16[256,2,512]{2,1,0:T(2,128)(2,1)S(1)}, u32[]{:S(2)}, u32[]{:S(2)}) %all-to-all-start) | async-done | bytes 524320 | tf_op jit(solution)/shard_map/all_to_all | solution.py:299
  163.3 0.4 convert_bitcast_fusion
  163.6 1.6 copy.7
  (4 shorter events, 0.2 us)
Async XLA Ops:
  0.6 1.6 copy-start
  38.3 36.2 %collective-permute-start = (bf16[4,256,512]{2,1,0:T(8,128)(2,1)S(1)}, bf16[4,256,512]{2,1,0:T(8,128)(2,1)S(1)}, u32[]{:S(2)}, u32[]{:S(2)}) collective-permute-start(bf16[4,256,512]{2,1,0:T(8,128)(2,1)S(1)} %get-tuple-element.30), channel_id=1, source_target_pairs={{0,4},{4,0},{8,12},{12,8},{16,20},{20,16},{24,28},{28,24},{1,5},{5... | collective-permute-start | bytes 3145736 | tf_op jit(solution)/shard_map/ppermute | solution.py:304
  74.0 40.5 %collective-permute-start.4 = (bf16[4,256,512]{2,1,0:T(8,128)(2,1)S(1)}, bf16[4,256,512]{2,1,0:T(8,128)(2,1)S(1)}, u32[]{:S(2)}, u32[]{:S(2)}) collective-permute-start(bf16[4,256,512]{2,1,0:T(8,128)(2,1)S(1)} %get-tuple-element.38), channel_id=1, source_target_pairs={{0,4},{4,0},{8,12},{12,8},{16,20},{20,16},{24,28},{28,24},{1,5},{5... | collective-permute-start | bytes 3145736 | tf_op jit(solution)/shard_map/ppermute | solution.py:304
  75.1 39.9 %collective-permute-start.1 = (bf16[256,512]{1,0:T(8,128)(2,1)S(1)}, bf16[256,512]{1,0:T(8,128)(2,1)S(1)}, u32[]{:S(2)}, u32[]{:S(2)}) collective-permute-start(bf16[256,512]{1,0:T(8,128)(2,1)S(1)} %get-tuple-element.34), channel_id=1, source_target_pairs={{0,8},{4,12},{8,16},{12,20},{16,24},{20,28},{24,0},{28,4},{1,9},{5... | collective-permute-start | bytes 786440 | tf_op jit(solution)/shard_map/ppermute | solution.py:313
  76.7 38.3 %collective-permute-start.2 = (bf16[256,512]{1,0:T(8,128)(2,1)S(1)}, bf16[256,512]{1,0:T(8,128)(2,1)S(1)}, u32[]{:S(2)}, u32[]{:S(2)}) collective-permute-start(bf16[256,512]{1,0:T(8,128)(2,1)S(1)} %get-tuple-element.35), channel_id=1, source_target_pairs={{0,16},{4,20},{8,24},{12,28},{16,0},{20,4},{24,8},{28,12},{1,17},{... | collective-permute-start | bytes 786440 | tf_op jit(solution)/shard_map/ppermute | solution.py:313
  79.3 35.7 %collective-permute-start.3 = (bf16[256,512]{1,0:T(8,128)(2,1)S(1)}, bf16[256,512]{1,0:T(8,128)(2,1)S(1)}, u32[]{:S(2)}, u32[]{:S(2)}) collective-permute-start(bf16[256,512]{1,0:T(8,128)(2,1)S(1)} %get-tuple-element.36), channel_id=1, source_target_pairs={{0,24},{4,28},{8,0},{12,4},{16,8},{20,12},{24,16},{28,20},{1,25},{... | collective-permute-start | bytes 786440 | tf_op jit(solution)/shard_map/ppermute | solution.py:313
  115.2 25.4 %collective-permute-start.5 = (bf16[256,512]{1,0:T(8,128)(2,1)S(1)}, bf16[256,512]{1,0:T(8,128)(2,1)S(1)}, u32[]{:S(2)}, u32[]{:S(2)}) collective-permute-start(bf16[256,512]{1,0:T(8,128)(2,1)S(1)} %get-tuple-element.42), channel_id=1, source_target_pairs={{0,8},{4,12},{8,16},{12,20},{16,24},{20,28},{24,0},{28,4},{1,9},{5... | collective-permute-start | bytes 786440 | tf_op jit(solution)/shard_map/ppermute | solution.py:313
  116.1 24.5 %collective-permute-start.6 = (bf16[256,512]{1,0:T(8,128)(2,1)S(1)}, bf16[256,512]{1,0:T(8,128)(2,1)S(1)}, u32[]{:S(2)}, u32[]{:S(2)}) collective-permute-start(bf16[256,512]{1,0:T(8,128)(2,1)S(1)} %get-tuple-element.43), channel_id=1, source_target_pairs={{0,16},{4,20},{8,24},{12,28},{16,0},{20,4},{24,8},{28,12},{1,17},{... | collective-permute-start | bytes 786440 | tf_op jit(solution)/shard_map/ppermute | solution.py:313
  118.9 21.8 %collective-permute-start.7 = (bf16[256,512]{1,0:T(8,128)(2,1)S(1)}, bf16[256,512]{1,0:T(8,128)(2,1)S(1)}, u32[]{:S(2)}, u32[]{:S(2)}) collective-permute-start(bf16[256,512]{1,0:T(8,128)(2,1)S(1)} %get-tuple-element.44), channel_id=1, source_target_pairs={{0,24},{4,28},{8,0},{12,4},{16,8},{20,12},{24,16},{28,20},{1,25},{... | collective-permute-start | bytes 786440 | tf_op jit(solution)/shard_map/ppermute | solution.py:313
  143.5 19.8 %all-to-all-start = ((bf16[256,2,512]{2,1,0:T(2,128)(2,1)}), bf16[256,2,512]{2,1,0:T(2,128)(2,1)S(1)}, u32[]{:S(2)}, u32[]{:S(2)}) async-start(bf16[256,2,512]{2,1,0:T(2,128)(2,1)} %copy.5), calls=%async_computation | async-start | bytes 1048576 | tf_op jit(solution)/shard_map/all_to_all | solution.py:299
